TPU v7x, 32 devices: a whole 2x2x4 slice. The times are simulated.
32 devices in a mesh: rep: 4 (over z), fsdp: 8 (over y, x, core).
Axes of the slice: x: 2, y: 2, z: 4, core: 2. Of those that a mesh axis runs over, the one named last changes fastest.
Arguments:
- layer_input: bfloat16 [16, 1024, 768], P('rep', 'fsdp'), may hold values from -40 to 40
- positions: int32 [16, 1024], P('rep', 'fsdp'), may hold values from 0 to 1023, as said below
- cotangent: bfloat16 [16, 1024, 768], P('rep', 'fsdp'), may hold values from -6 to 6
- w_qkv: bfloat16 [768, 2304], P('fsdp'), may hold values from -4 to 4
- w_out: bfloat16 [768, 768], P('fsdp'), may hold values from -1.75 to 1.75
- w_up: bfloat16 [768, 3072], P('fsdp'), may hold values from -0.21875 to 0.21875
- w_down: bfloat16 [768, 3072], P('fsdp'), may hold values from -0.109375 to 0.109375
- ln1_gain: bfloat16 [768], P('fsdp'), may hold values from 0.5 to 1.5
- ln1_bias: bfloat16 [768], P('fsdp'), may hold values from -1.5 to 1.5
- ln2_gain: bfloat16 [768], P('fsdp'), may hold values from 0.5 to 1.5
- ln2_bias: bfloat16 [768], P('fsdp'), may hold values from -1.5 to 1.5
- qkv_bias: bfloat16 [2304], P('fsdp'), may hold values from -2.5 to 2.5
- out_bias: bfloat16 [768], P('fsdp'), may hold values from -2.5 to 2.5
- up_bias: bfloat16 [3072], P('fsdp'), may hold values from -2.5 to 2.5
- down_bias: bfloat16 [768], P('fsdp'), may hold values from -2.5 to 2.5
Outputs:
- output: bfloat16 [16, 1024, 768], P('rep', 'fsdp')
- grad_input: bfloat16 [16, 1024, 768], P('rep', 'fsdp')
- grad_w_qkv: float32 [768, 2304], P('fsdp')
- grad_w_out: float32 [768, 768], P('fsdp')
- grad_w_up: float32 [768, 3072], P('fsdp')
- grad_w_down: float32 [768, 3072], P('fsdp')
- grad_ln1_gain: float32 [768], P('fsdp')
- grad_ln1_bias: float32 [768], P('fsdp')
- grad_ln2_gain: float32 [768], P('fsdp')
- grad_ln2_bias: float32 [768], P('fsdp')
- grad_qkv_bias: float32 [2304], P('fsdp')
- grad_out_bias: float32 [768], P('fsdp')
- grad_up_bias: float32 [3072], P('fsdp')
- grad_down_bias: float32 [768], P('fsdp')
Inputs may be any that keep to these rules, and one draw needn't show every extreme that they name: positions[s, 0] is 0, and each later positions[s, t] is either 0 or positions[s, t - 1] + 1; sequence 0 is one document of 1024 tokens.
All inputs are finite; a program needn't handle non-finite values.
Results may differ from a plain program's by a relative error of at most 0.0093.
Values may be sent and summed in bfloat16 or wider, within the bound.
No kernel may reach another device: no remote copies, remote signals or barrier semaphores. Data moves between devices by JAX's collectives and lax.ppermute only.
A program may use at most 320 MiB of HBM per device.

v0:
```python
import jax
import jax.numpy as jnp
from jax import lax
from jax.sharding import PartitionSpec as P

H = 12
HD = 64
ROT = 16
EPS = 1e-05
NEG = -1e30


def norm_rows(values, gain, shift):
    mean = jnp.mean(values, axis=-1, keepdims=True)
    centred = values - mean
    spread = jnp.mean(centred * centred, axis=-1, keepdims=True)
    return centred * lax.rsqrt(spread + EPS) * gain + shift


def rotate(values, cosine, sine):
    half = ROT // 2
    head = values[..., :ROT]
    turned = jnp.concatenate([-head[..., half:], head[..., :half]], axis=-1)
    return jnp.concatenate([head * cosine + turned * sine, values[..., ROT:]], axis=-1)


def angles(positions):
    inverse = 10000.0 ** (-jnp.arange(0, ROT, 2, dtype=jnp.float32) / ROT)
    phase = positions.astype(jnp.float32)[..., None] * inverse
    phase = jnp.concatenate([phase, phase], axis=-1)[..., None, :]
    return (jnp.cos(phase), jnp.sin(phase))


def on_device(
    layer_input,
    positions,
    cotangent,
    w_qkv,
    w_out,
    w_up,
    w_down,
    ln1_gain,
    ln1_bias,
    ln2_gain,
    ln2_bias,
    qkv_bias,
    out_bias,
    up_bias,
    down_bias,
):
    seq_count, span_len, width = layer_input.shape
    shard_count = lax.axis_size("fsdp")
    shard_index = lax.axis_index("fsdp")
    row_count = seq_count * span_len
    qkv_cols = w_qkv.shape[1]
    hidden_cols = w_up.shape[1]
    vectors = (
        lax.all_gather(ln1_gain, "fsdp", axis=0, tiled=True),
        lax.all_gather(ln1_bias, "fsdp", axis=0, tiled=True),
        lax.all_gather(ln2_gain, "fsdp", axis=0, tiled=True),
        lax.all_gather(ln2_bias, "fsdp", axis=0, tiled=True),
        lax.all_gather(qkv_bias, "fsdp", axis=0, tiled=True),
        lax.all_gather(out_bias, "fsdp", axis=0, tiled=True),
        lax.all_gather(up_bias, "fsdp", axis=0, tiled=True),
        lax.all_gather(down_bias, "fsdp", axis=0, tiled=True),
    )
    gain_one, shift_one, gain_two, shift_two, bias_qkv, bias_out, bias_up, bias_down = [
        v.astype(jnp.float32) for v in vectors
    ]
    source = layer_input.reshape(row_count, width).astype(jnp.float32)
    normed_one, pull_one = jax.vjp(norm_rows, source, gain_one, shift_one)
    normed_two, pull_two = jax.vjp(norm_rows, source, gain_two, shift_two)
    input_one = normed_one.astype(jnp.bfloat16)
    input_two = normed_two.astype(jnp.bfloat16)
    pieces = (
        lax.all_gather(w_qkv, "fsdp", axis=0, tiled=True),
        lax.all_gather(w_up, "fsdp", axis=0, tiled=True),
    )
    count = pieces[0].shape[0]
    qkv_sum = jnp.dot(input_one, pieces[0], preferred_element_type=jnp.float32)
    up_sum = jnp.dot(input_two, pieces[1], preferred_element_type=jnp.float32)
    qkv_full = qkv_sum + bias_qkv
    up_full = up_sum + bias_up
    cosine, sine = angles(positions)

    def turn_all(packed):
        shaped = packed.reshape(seq_count, span_len, 3, H, HD)
        return (
            rotate(shaped[:, :, 0], cosine, sine),
            rotate(shaped[:, :, 1], cosine, sine),
            shaped[:, :, 2],
        )

    turned, pull_turn = jax.vjp(turn_all, qkv_full)
    query_low = turned[0].astype(jnp.bfloat16)
    key_low = turned[1].astype(jnp.bfloat16)
    value_low = turned[2].astype(jnp.bfloat16)
    key_flat = key_low.reshape(seq_count, span_len, width)
    value_flat = value_low.reshape(seq_count, span_len, width)
    query_index = shard_index * span_len + jnp.arange(span_len, dtype=jnp.int32)
    first_seen = query_index[None, :] - positions

    def scores_with(key_piece):
        count = key_piece.shape[1]
        keys = key_piece.reshape(seq_count, count, H, HD)
        raw = (
            jnp.einsum("sqhd,skhd->shqk", query_low, keys, preferred_element_type=jnp.float32)
            * 0.125
        )
        key_index = jnp.arange(count, dtype=jnp.int32)
        seen = (key_index[None, None, :] <= query_index[None, :, None]) & (
            key_index[None, None, :] >= first_seen[:, :, None]
        )
        return (raw, seen[:, None])

    start_top = jnp.full((seq_count, H, span_len), NEG, jnp.float32)
    raw, seen = scores_with(lax.all_gather(key_flat, "fsdp", axis=1, tiled=True))
    masked = jnp.where(seen, raw, NEG)
    new_top = jnp.maximum(start_top, jnp.max(masked, axis=-1))
    weights = jnp.where(seen, jnp.exp(masked - new_top[..., None]), 0.0)
    total = jnp.sum(weights, axis=-1)
    log_total = new_top + jnp.log(total)
    pieces = (
        lax.all_gather(key_flat, "fsdp", axis=1, tiled=True),
        lax.all_gather(value_flat, "fsdp", axis=1, tiled=True),
    )
    raw, seen = scores_with(pieces[0])
    count = pieces[1].shape[1]
    values = pieces[1].reshape(seq_count, count, H, HD)
    probs = jnp.where(seen, jnp.exp(raw - log_total[..., None]), 0.0)
    probs_low = probs.astype(jnp.bfloat16)
    residue = (probs - probs_low.astype(jnp.float32)).astype(jnp.bfloat16)
    mixed_sum = jnp.einsum("shqk,skhd->sqhd", probs_low, values, preferred_element_type=jnp.float32)
    residue_sum = jnp.einsum("shqk,skhd->sqhd", residue, values, preferred_element_type=jnp.float32)
    attended = mixed_sum.reshape(row_count, width).astype(jnp.bfloat16)
    hidden = jax.nn.gelu(up_full, approximate=False).astype(jnp.bfloat16)
    pieces = (
        lax.all_gather(w_out, "fsdp", axis=0, tiled=True),
        lax.all_gather(w_down, "fsdp", axis=0, tiled=True),
    )
    columns = jnp.einsum("rk,ck->rc", attended, pieces[0], preferred_element_type=jnp.float32)
    columns = columns + jnp.einsum(
        "rk,ck->rc", hidden, pieces[1], preferred_element_type=jnp.float32
    )
    output = (
        (source + columns + bias_out + bias_down).astype(jnp.bfloat16).reshape(layer_input.shape)
    )
    grad_out = cotangent.reshape(row_count, width)
    pieces = (
        lax.all_gather(w_out, "fsdp", axis=0, tiled=True),
        lax.all_gather(w_down, "fsdp", axis=0, tiled=True),
    )
    count = pieces[0].shape[0]
    grad_attended = jnp.dot(grad_out, pieces[0], preferred_element_type=jnp.float32)
    grad_hidden = jnp.dot(grad_out, pieces[1], preferred_element_type=jnp.float32)
    grad_mixed = grad_attended.astype(jnp.bfloat16)
    gelu_value, pull_gelu = jax.vjp(lambda v: jax.nn.gelu(v, approximate=False), up_full)
    grad_up = pull_gelu(grad_hidden)[0].astype(jnp.bfloat16)
    grad_heads = grad_mixed.reshape(seq_count, span_len, H, HD)
    carried = jnp.sum(grad_heads.astype(jnp.float32) * (mixed_sum + residue_sum), axis=-1)
    carried_rows = jnp.transpose(carried, (0, 2, 1))
    pieces = (
        lax.all_gather(key_flat, "fsdp", axis=1, tiled=True),
        lax.all_gather(value_flat, "fsdp", axis=1, tiled=True),
    )
    raw, seen = scores_with(pieces[0])
    count = pieces[0].shape[1]
    keys = pieces[0].reshape(seq_count, count, H, HD)
    values = pieces[1].reshape(seq_count, count, H, HD)
    probs = jnp.where(seen, jnp.exp(raw - log_total[..., None]), 0.0)
    probs_low = probs.astype(jnp.bfloat16)
    grad_probs = jnp.einsum(
        "sqhd,skhd->shqk", grad_heads, values, preferred_element_type=jnp.float32
    )
    grad_scores = (probs * (grad_probs - carried_rows[..., None])).astype(jnp.bfloat16)
    grad_query = jnp.einsum(
        "shqk,skhd->sqhd", grad_scores, keys, preferred_element_type=jnp.float32
    )
    key_part = jnp.einsum(
        "shqk,sqhd->skhd", grad_scores, query_low, preferred_element_type=jnp.float32
    )
    value_part = jnp.einsum(
        "shqk,sqhd->skhd", probs_low, grad_heads, preferred_element_type=jnp.float32
    )
    both = jnp.concatenate(
        [key_part.reshape(seq_count, count, width), value_part.reshape(seq_count, count, width)],
        axis=2,
    )
    key_terms = both
    grad_query, key_terms = (grad_query, key_terms)
    grad_query = grad_query * 0.125
    key_owned = lax.psum_scatter(key_terms, "fsdp", scatter_dimension=1, tiled=True)
    grad_key = key_owned[..., :width].reshape(seq_count, span_len, H, HD) * 0.125
    grad_value = key_owned[..., width:].reshape(seq_count, span_len, H, HD)
    grad_qkv = pull_turn((grad_query, grad_key, grad_value))[0].astype(jnp.bfloat16)
    pieces = (
        lax.all_gather(w_qkv, "fsdp", axis=0, tiled=True),
        lax.all_gather(w_up, "fsdp", axis=0, tiled=True),
    )
    columns_one = jnp.einsum("rk,ck->rc", grad_qkv, pieces[0], preferred_element_type=jnp.float32)
    columns_two = jnp.einsum("rk,ck->rc", grad_up, pieces[1], preferred_element_type=jnp.float32)
    grad_source_one, grad_gain_one, grad_shift_one = pull_one(columns_one)
    grad_source_two, grad_gain_two, grad_shift_two = pull_two(columns_two)
    grad_out_float = grad_out.astype(jnp.float32)
    grad_input = (
        (grad_out_float + grad_source_one + grad_source_two)
        .astype(jnp.bfloat16)
        .reshape(layer_input.shape)
    )
    grad_out_total = jnp.sum(grad_out_float, axis=0)
    local_vectors = (
        grad_gain_one,
        grad_shift_one,
        grad_gain_two,
        grad_shift_two,
        jnp.sum(grad_qkv.astype(jnp.float32), axis=0),
        grad_out_total,
        jnp.sum(grad_up.astype(jnp.float32), axis=0),
    )
    summed = lax.psum(
        (
            local_vectors[0],
            local_vectors[1],
            local_vectors[2],
            local_vectors[3],
            local_vectors[4],
            local_vectors[5],
            local_vectors[6],
        ),
        ("rep", "fsdp"),
    )
    owned_vectors = [
        lax.dynamic_slice_in_dim(
            v, shard_index * (v.shape[0] // shard_count), v.shape[0] // shard_count
        )
        for v in summed
    ]
    owned = lax.psum_scatter(
        jnp.concatenate(
            [
                jnp.einsum("rc,rk->ck", input_one, grad_qkv, preferred_element_type=jnp.float32),
                jnp.einsum("rc,rk->ck", grad_out, attended, preferred_element_type=jnp.float32),
                jnp.einsum("rc,rk->ck", input_two, grad_up, preferred_element_type=jnp.float32),
                jnp.einsum("rc,rk->ck", grad_out, hidden, preferred_element_type=jnp.float32),
            ],
            axis=1,
        ),
        "fsdp",
        scatter_dimension=0,
        tiled=True,
    )
    owned = lax.psum(owned, "rep")
    edge_two = qkv_cols + width
    edge_three = edge_two + hidden_cols
    grad_w_qkv = owned[:, :qkv_cols]
    grad_w_out = owned[:, qkv_cols:edge_two]
    grad_w_up = owned[:, edge_two:edge_three]
    grad_w_down = owned[:, edge_three:]
    return (
        output,
        grad_input,
        grad_w_qkv,
        grad_w_out,
        grad_w_up,
        grad_w_down,
        owned_vectors[0],
        owned_vectors[1],
        owned_vectors[2],
        owned_vectors[3],
        owned_vectors[4],
        owned_vectors[5],
        owned_vectors[6],
        owned_vectors[5],
    )


def solution(mesh):
    return jax.shard_map(
        on_device,
        mesh=mesh,
        in_specs=(
            P("rep", "fsdp", None),
            P("rep", "fsdp"),
            P("rep", "fsdp", None),
            P("fsdp", None),
            P("fsdp", None),
            P("fsdp", None),
            P("fsdp", None),
            P("fsdp"),
            P("fsdp"),
            P("fsdp"),
            P("fsdp"),
            P("fsdp"),
            P("fsdp"),
            P("fsdp"),
            P("fsdp"),
        ),
        out_specs=(
            P("rep", "fsdp", None),
            P("rep", "fsdp", None),
            P("fsdp", None),
            P("fsdp", None),
            P("fsdp", None),
            P("fsdp", None),
            P("fsdp"),
            P("fsdp"),
            P("fsdp"),
            P("fsdp"),
            P("fsdp"),
            P("fsdp"),
            P("fsdp"),
            P("fsdp"),
        ),
        check_vma=False,
    )
```

profile of v0, /device:TPU:0, one launch (start us, length us, event | category | flops | bytes accessed | tf_op | source)
XLA Modules:
  0.0 780.7 jit_solution(14124956346842506521)
XLA Ops:
  21.0 26.5 %all-reduce.19 = (bf16[768]{0:T(1024)(128)(2,1)S(1)}, bf16[768]{0:T(1024)(128)(2,1)S(1)}, bf16[768]{0:T(1024)(128)(2,1)}, bf16[768]{0:T(1024)(128)(2,1)}, bf16[7...) all-reduce(bf16[768]{0:T(1024)(128)(2,1)S(1)} %dynamic-update-slice, ...), channel_id=1, replica_groups=mesh['rep'=4,'fsdp'=8] {'fsdp'}, use_global_device_ids=true, to_apply=%add.15 | all-reduce | flops 6912 | bytes 27648
  49.2 6.1 convolution_add_fusion
  55.4 6.2 copy.46
  61.5 6.3 reshape.249
  84.6 37.4 %all-gather.12.cloned.1.call-done = bf16[4,1024,768]{1,2,0:T(8,128)(2,1)} async-done(((bf16[4,128,768]{1,2,0:T(8,128)(2,1)}), bf16[4,1024,768]{1,2,0:T(8,128)(2,1)}) %all-gather.12.cloned.1.call-update) | async-done | bytes 6291472 | tf_op jit(solution)/shard_map/all_gather | solution.py:124
  121.9 12.9 %select_reduce_fusion.1 = (f32[4,12,128]{2,1,0:T(8,128)S(1)}, f32[4,12,128,1024]{3,2,1,0:T(8,128)}) fusion(pred[4,128,1024]{2,1,0:T(8,128)(4,1)S(1)} %fusion.13, bf16[4,1024,12,64]{1,3,2,0:T(8,128)(2,1)} %bitcast.164, bf16[4,128,12,48]{1,3,2,0:T(8,128)(2,1)S(1)} %slice.110, bf16[4,128,12,16]{1,3,2,0:T(8,128)(2,1)S(1)} %get-tuple-element.61), kind=kOutput, calls=%fused_computation.6 | convolution fusion | flops 825747456 | bytes 32792576 | tf_op jit(solution)/shard_map/sqhd,skhd->shqk/dot_general | solution.py:107
  134.9 12.2 %select_reduce_fusion = f32[4,12,128]{2,1,0:T(8,128)S(1)} fusion(f32[4,12,128,1024]{3,2,1,0:T(8,128)} %get-tuple-element.76, f32[4,12,128]{2,1,0:T(8,128)S(1)} %broadcast_maximum_fusion, pred[4,128,1024]{2,1,0:T(8,128)(4,1)S(1)} %fusion.13), kind=kLoop, calls=%fused_computation.5 | loop fusion | flops 31451136 | bytes 25739264 | tf_op jit(solution)/shard_map/reduce_sum | solution.py:121
  147.1 23.9 %all-gather.10.cloned.1.call-done = bf16[4,1024,768]{1,2,0:T(8,128)(2,1)} async-done(((bf16[4,128,768]{1,2,0:T(8,128)(2,1)}), bf16[4,1024,768]{1,2,0:T(8,128)(2,1)}) %all-gather.10.cloned.1.call-update) | async-done | bytes 6291472 | tf_op jit(solution)/shard_map/all_gather | solution.py:125
  170.9 14.2 %fusion.58 = f32[4,12,64,128]{3,2,1,0:T(8,128)} fusion(bf16[4,1024,12,64]{1,3,2,0:T(8,128)(2,1)} %bitcast.190, f32[4,12,128,1024]{3,2,1,0:T(8,128)} %get-tuple-element.76, f32[4,12,128]{2,1,0:T(8,128)S(1)} %log_add_fusion, pred[4,128,1024]{2,1,0:T(8,128)(4,1)S(1)} %fusion.13), kind=kOutput, calls=%fused_computation.110 | convolution fusion | flops 830472192 | bytes 33579008 | tf_op jit(solution)/shard_map/shqk,skhd->sqhd/dot_general | solution.py:133
  185.2 15.0 %fusion.16 = f32[4,128,12]{1,2,0:T(8,128)S(1)} fusion(f32[4,12,64,128]{3,2,1,0:T(8,128)} %fusion.58, bf16[4,1024,12,64]{1,3,2,0:T(8,128)(2,1)} %bitcast.191, f32[4,12,128,1024]{3,2,1,0:T(8,128)} %get-tuple-element.76, f32[4,12,128]{2,1,0:T(8,128)S(1)} %log_add_fusion, pred[4,128,1024]{2,1,0:T(8,128)(4,1)S(1)} %fusion.13, bf16[4,128,12,64]{1,0,3,2:T(4,128)(2,1)} %reshape.254), kind=kOutput, calls=%fused_computation.48 | convolution fusion | flops 850913280 | bytes 34390016 | tf_op jit(solution)/shard_map/shqk,skhd->sqhd/dot_general | solution.py:134
  200.2 20.5 %multiply_convert_fusion = bf16[4,12,128,1024]{3,2,1,0:T(8,128)(2,1)} fusion(f32[4,12,128,1024]{3,2,1,0:T(8,128)} %get-tuple-element.76, f32[4,12,128]{2,1,0:T(8,128)S(1)} %bitcast.194, f32[4,12,128]{2,1,0:T(8,128)S(1)} %log_add_fusion, pred[4,128,1024]{2,1,0:T(8,128)(4,1)S(1)} %fusion.13, bf16[4,1024,12,64]{1,3,2,0:T(8,128)(2,1)} %bitcast.192, ...), kind=kOutput, calls=%fused_computation.2 | convolution fusion | flops 843055104 | bytes 45400064 | tf_op jit(solution)/shard_map/sqhd,skhd->shqk/dot_general | solution.py:172
  220.6 11.1 %fusion.50 = f32[4,12,64,1024]{3,2,1,0:T(8,128)} fusion(bf16[4,12,128,1024]{3,2,1,0:T(8,128)(2,1)} %multiply_convert_fusion, bf16[4,128,12,48]{1,3,2,0:T(8,128)(2,1)S(1)} %slice.110, bf16[4,128,12,16]{1,3,2,0:T(8,128)(2,1)S(1)} %get-tuple-element.61), kind=kOutput, calls=%fused_computation.98 | convolution fusion | flops 806879232 | bytes 25952256 | tf_op jit(solution)/shard_map/shqk,sqhd->skhd/dot_general | solution.py:179
  231.8 14.8 %fusion.47 = f32[4,12,64,1024]{3,2,1,0:T(8,128)} fusion(bf16[4,128,12,64]{1,0,3,2:T(4,128)(2,1)S(1)} %copy-done.12, f32[4,12,128,1024]{3,2,1,0:T(8,128)} %get-tuple-element.76, f32[4,12,128]{2,1,0:T(8,128)S(1)} %log_add_fusion, pred[4,128,1024]{2,1,0:T(8,128)(4,1)S(1)} %fusion.13), kind=kOutput, calls=%fused_computation.94 | convolution fusion | flops 830472192 | bytes 39084032 | tf_op jit(solution)/shard_map/shqk,sqhd->skhd/dot_general | solution.py:182
  246.5 18.8 %pad_maximum_fusion.1 = f32[4,1024,1536]{1,2,0:T(8,128)} fusion(f32[4,1024,768]{1,2,0:T(8,128)} %bitcast.163, f32[4,1024,768]{1,2,0:T(8,128)} %bitcast.162), kind=kLoop, calls=%fused_computation.1 | loop fusion | flops 6291456 | bytes 50331648 | tf_op jit(solution)/shard_map/concatenate | solution.py:185
  266.0 9.4 %all-gather = bf16[8,1,384]{2,1,0:T(2,128)(2,1)S(1)} all-gather(bf16[1,1,384]{2,1,0:T(2,128)(2,1)S(1)} %reshape.280), channel_id=1, replica_groups=mesh['rep'=4,'fsdp'=8] {'fsdp'}, dimensions={0}, use_global_device_ids=true | all-gather | bytes 6912 | tf_op jit(solution)/shard_map/all_gather | solution.py:64
  276.7 8.9 %fusion.83 = f32[512,3072]{1,0:T(8,128)} fusion(bf16[512,768]{1,0:T(8,128)(2,1)S(1)} %get-tuple-element.54, bf16[768,3072]{1,0:T(8,128)(2,1)} %all-gather.16.cloned.1.call-done), kind=kOutput, calls=%fused_computation.154 | convolution fusion | flops 2415919104 | bytes 11796480 | tf_op jit(solution)/shard_map/dot_general | solution.py:81
  285.6 19.4 %convert_reduce_fusion = (f32[3072]{0:T(1024)S(1)}, bf16[512,3072]{1,0:T(8,128)(2,1)S(1)}, f32[512,3072]{1,0:T(8,128)S(1)}) fusion(f32[512,3072]{1,0:T(8,128)} %fusion.83, f32[3072]{0:T(1024)S(1)} %bitcast.188, bf16[512,768]{1,0:T(8,128)(2,1)S(1)} %bitcast.170, bf16[768,3072]{1,0:T(8,128)(2,1)} %all-gather.18.cloned.1.call-done), kind=kOutput, calls=%fused_computation.12 | convolution fusion | flops 2533880832 | bytes 21258240 | tf_op jit(solution)/shard_map/dot_general | solution.py:155
  308.2 7.8 convolution_bitcast_fusion
  321.2 11.3 %multiply_bitcast_fusion = f32[4,128,12,64]{1,3,2,0:T(8,128)S(1)} fusion(bf16[4,1024,12,64]{1,3,2,0:T(8,128)(2,1)} %bitcast.165, bf16[4,12,128,1024]{3,2,1,0:T(8,128)(2,1)} %multiply_convert_fusion), kind=kOutput, calls=%fused_computation.82 | convolution fusion | flops 805699584 | bytes 20447232 | tf_op jit(solution)/shard_map/shqk,skhd->sqhd/dot_general | solution.py:176
  340.6 82.4 %reduce-scatter.3.cloned.1.call-done = f32[4,128,1536]{1,2,0:T(8,128)} async-done(((f32[4,1024,1536]{1,2,0:T(8,128)}), f32[4,128,1536]{1,2,0:T(8,128)}) %reduce-scatter.3.cloned.1.call-update) | async-done | bytes 3145744 | tf_op jit(solution)/shard_map/reduce_scatter | solution.py:192
  436.1 19.4 %pad_maximum_fusion = f32[768,9216]{1,0:T(8,128)} fusion(f32[768,3072]{1,0:T(8,128)} %convolution_bitcast_fusion, f32[768,3072]{1,0:T(8,128)} %fusion.86, f32[768,768]{1,0:T(8,128)S(1)} %copy.57, f32[768,2304]{1,0:T(8,128)} %fusion.9), kind=kLoop, calls=%fused_computation | loop fusion | flops 21233664 | bytes 56623104 | tf_op jit(solution)/shard_map/concatenate | solution.py:239
  456.4 172.6 %reduce-scatter.5.cloned.1.call-done = f32[96,9216]{1,0:T(8,128)} async-done(((f32[768,9216]{1,0:T(8,128)}), f32[96,9216]{1,0:T(8,128)}) %reduce-scatter.5.cloned.1.call-update) | async-done | bytes 3538960 | tf_op jit(solution)/shard_map/reduce_scatter | solution.py:238
  650.8 44.4 %all-reduce.18 = (f32[768]{0:T(1024)S(1)}, f32[768]{0:T(1024)S(1)}, f32[768]{0:T(1024)S(1)}, f32[768]{0:T(1024)S(1)}, f32[2304]{0:T(1024)S(1)}, /*index=5*/f32[768]{0:T(1024)S(1)}, f32[3072]{0:T(1024)S(1)}) all-reduce(f32[768]{0:T(1024)S(1)} %get-tuple-element.23, ...), channel_id=1, replica_groups=mesh['rep'=4,'fsdp'=8] {'rep','fsdp'}, use_global_device_ids=true, to_apply=%region_13.14 | all-reduce | flops 9216 | bytes 73728 | tf_op jit(solution)/shard_map/psum | solution.py:220
  701.9 64.2 %all-reduce.22.cloned.1.call-done = f32[96,9216]{1,0:T(8,128)} async-done(((f32[96,9216]{1,0:T(8,128)}), f32[96,9216]{1,0:T(8,128)}) %all-reduce.22.cloned.1.call-update) | async-done | bytes 3538960 | tf_op jit(solution)/shard_map/psum | solution.py:252
  (184 shorter events, 98.8 us)
Async XLA Ops:
  7.2 42.0 %all-gather.8.cloned.1.call-start = ((), (), s32[]{:S(2)}) async-start(), calls=%async_computation.2 | async-start | bytes 3981312 | tf_op jit(solution)/shard_map/all_gather | solution.py:76
  7.9 69.8 %all-gather.14.cloned.1.call-start = ((), (), s32[]{:S(2)}) async-start(), calls=%async_computation.5 | async-start | bytes 1327104 | tf_op jit(solution)/shard_map/all_gather | solution.py:138
  8.7 113.3 %all-gather.12.cloned.1.call-start = ((), (), s32[]{:S(2)}) async-start(), calls=%async_computation.4 | async-start | bytes 7077888 | tf_op jit(solution)/shard_map/all_gather | solution.py:124
  10.0 45.3 %copy-start.23 = (f32[512]{0:T(512)}, f32[512]{0:T(512)S(1)}, u32[]{:S(2)}) copy-start(f32[512]{0:T(512)S(1)} %get-tuple-element.73) | copy-start | bytes 6148
  11.6 263.9 %copy-start.27 = (f32[4,128]{1,0:T(4,128)}, f32[4,128]{1,0:T(4,128)S(1)}, u32[]{:S(2)}) copy-start(f32[4,128]{1,0:T(4,128)S(1)} %fusion.28) | copy-start | bytes 6148
  12.5 58.2 %copy-start.15 = (f32[4,128,16]{1,2,0:T(8,128)}, f32[4,128,16]{1,2,0:T(8,128)S(1)}, u32[]{:S(2)}) copy-start(f32[4,128,16]{1,2,0:T(8,128)S(1)} %get-tuple-element.67) | copy-start | bytes 98308
  12.5 58.2 %copy-start.17 = (f32[4,128,16]{1,2,0:T(8,128)}, f32[4,128,16]{1,2,0:T(8,128)S(1)}, u32[]{:S(2)}) copy-start(f32[4,128,16]{1,2,0:T(8,128)S(1)} %get-tuple-element.68) | copy-start | bytes 98308
  47.5 228.0 %copy-start.19 = (f32[768]{0:T(1024)}, f32[768]{0:T(1024)S(1)}, u32[]{:S(2)}) copy-start(f32[768]{0:T(1024)S(1)} %convert_element_type.126) | copy-start | bytes 9220
  47.5 7.9 %copy-start.21 = (f32[768]{0:T(1024)}, f32[768]{0:T(1024)S(1)}, u32[]{:S(2)}) copy-start(f32[768]{0:T(1024)S(1)} %convert_element_type.137) | copy-start | bytes 9220
  47.6 7.8 copy-start.25
  72.8 98.1 %all-gather.10.cloned.1.call-start = ((), (), s32[]{:S(2)}) async-start(), calls=%async_computation.3 | async-start | bytes 7077888 | tf_op jit(solution)/shard_map/all_gather | solution.py:125
  75.6 201.1 %all-gather.16.cloned.1.call-start = ((), (), s32[]{:S(2)}) async-start(), calls=%async_computation.6 | async-start | bytes 5308416 | tf_op jit(solution)/shard_map/all_gather | solution.py:77
  76.2 209.3 %all-gather.18.cloned.1.call-start = ((), (), s32[]{:S(2)}) async-start(), calls=%async_computation.7 | async-start | bytes 5308416 | tf_op jit(solution)/shard_map/all_gather | solution.py:139
  76.8 346.2 %reduce-scatter.3.cloned.1.call-start = ((), (), s32[]{:S(2)}) async-start(), calls=%async_computation.8 | async-start | bytes 28311552 | tf_op jit(solution)/shard_map/reduce_scatter | solution.py:192
  220.6 11.1 %copy-start.12 = (bf16[4,128,12,64]{1,0,3,2:T(4,128)(2,1)S(1)}, bf16[4,128,12,64]{1,0,3,2:T(4,128)(2,1)}, u32[]{:S(2)}) copy-start(bf16[4,128,12,64]{1,0,3,2:T(4,128)(2,1)} %reshape.254) | copy-start | bytes 2359300
  265.3 10.1 %copy-start = (bf16[4,128,768]{2,1,0:T(8,128)(2,1)S(1)}, bf16[4,128,768]{2,1,0:T(8,128)(2,1)}, u32[]{:S(2)}) copy-start(bf16[4,128,768]{2,1,0:T(8,128)(2,1)} %param.15) | copy-start | bytes 2359300
  265.3 363.6 %reduce-scatter.5.cloned.1.call-start = ((), (), s32[]{:S(2)}) async-start(), calls=%async_computation.9 | async-start | bytes 31850496 | tf_op jit(solution)/shard_map/reduce_scatter | solution.py:238
  285.6 19.4 %copy-start.2 = (f32[512,3072]{1,0:T(8,128)S(1)}, f32[512,3072]{1,0:T(8,128)}, u32[]{:S(2)}) copy-start(f32[512,3072]{1,0:T(8,128)} %fusion.83) | copy-start | bytes 18874372
  305.0 11.0 %copy-start.8 = (bf16[512,3072]{1,0:T(8,128)(2,1)}, bf16[512,3072]{1,0:T(8,128)(2,1)S(1)}, u32[]{:S(2)}) copy-start(bf16[512,3072]{1,0:T(8,128)(2,1)S(1)} %get-tuple-element.39) | copy-start | bytes 9437188
  338.5 86.7 %copy-start.18 = (f32[4,128,16]{1,2,0:T(8,128)S(1)}, f32[4,128,16]{1,2,0:T(8,128)}, u32[]{:S(2)}) copy-start(f32[4,128,16]{1,2,0:T(8,128)} %copy-done.17) | copy-start | bytes 98308
  340.6 85.1 %copy-start.16 = (f32[4,128,16]{1,2,0:T(8,128)S(1)}, f32[4,128,16]{1,2,0:T(8,128)}, u32[]{:S(2)}) copy-start(f32[4,128,16]{1,2,0:T(8,128)} %copy-done.15) | copy-start | bytes 98308
  455.5 310.6 %all-reduce.22.cloned.1.call-start = ((), (), s32[]{:S(2)}) async-start(), calls=%async_computation.10 | async-start | bytes 7077888 | tf_op jit(solution)/shard_map/psum | solution.py:252
  642.9 6.5 copy-start.26
  695.3 78.0 %copy-start.33 = (f32[96]{0:T(128)}, f32[96]{0:T(128)S(1)}, u32[]{:S(2)}) copy-start(f32[96]{0:T(128)S(1)} %dynamic_slice.26) | copy-start | bytes 1156
  (20 other events, 58.3 us)
Sparse Core Ops, SparseCore 0:
  9.9 36.8 all-gather.7
  48.7 24.0 all-gather.13
  75.2 46.6 all-gather.11
  124.2 46.6 all-gather.9
  172.7 38.9 all-gather.15
  213.4 38.8 all-gather.17
  265.5 157.4 reduce-scatter.2
  455.7 173.2 reduce-scatter.4
  631.3 134.7 all-reduce.21
where the time goes:
time: 787 us; the launch traced here: 781 us
  waiting for transfers between devices  383 us (49%)
  matrix products  176 us (22%)
  blocking collectives  80.3 us (10%)
  other arithmetic  72.3 us (9%)
  local copies, waits for them, and re-layouts  51.7 us (7%)
  between operations  16.3 us (2%)
    reduce_scatter x1, waiting for transfers between devices, on_device(): lax.psum_scatter(jnp.concatenate([jnp.einsum('rc,rk->ck', input_one, grad...  173 us
    reduce_scatter x1, waiting for transfers between devices, on_device(): lax.psum_scatter(key_terms, 'fsdp', scatter_dimension=1, tiled=True)  82.4 us
    psum x1, waiting for transfers between devices, on_device(): owned = lax.psum(owned, 'rep')  64.2 us
    psum x1, blocking collectives, on_device(): lax.psum((local_vectors[0], local_vectors[1], local_vectors[2], local_vec...  44.4 us
    all_gather x1, waiting for transfers between devices, on_device(): lax.all_gather(key_flat, 'fsdp', axis=1, tiled=True)  37.4 us
    unnamed x1, blocking collectives  26.5 us
    all_gather x1, waiting for transfers between devices, on_device(): lax.all_gather(value_flat, 'fsdp', axis=1, tiled=True)  23.9 us
    dot_general x1, matrix products, on_device(): jnp.einsum('sqhd,skhd->shqk', grad_heads, values, preferred_element_type=...  20.5 us
  transfers between devices with their start and end apart: 9, of which 5 were waited for; matrix products, arithmetic and copies ran while one was open for 33% of the time, Pallas kernels for 0%

commit v1 on v0

--- a/solution.py
+++ b/solution.py
@@ -8,6 +8,17 @@
 ROT = 16
 EPS = 1e-05
 NEG = -1e30
+
+
+def ring_gather(x, axis, dim):
+    ways = lax.axis_size(axis)
+    pieces = [x]
+    for far in range(1, ways):
+        pieces.append(
+            lax.ppermute(pieces[far - 1], axis, [(d, (d - 1) % ways) for d in range(ways)])
+        )
+    line = jnp.concatenate(pieces, axis=dim)
+    return jnp.roll(line, lax.axis_index(axis) * x.shape[dim], axis=dim)
 
 
 def norm_rows(values, gain, shift):
@@ -121,7 +132,7 @@
     total = jnp.sum(weights, axis=-1)
     log_total = new_top + jnp.log(total)
     pieces = (
-        lax.all_gather(key_flat, "fsdp", axis=1, tiled=True),
+        ring_gather(key_flat, "fsdp", 1),
         lax.all_gather(value_flat, "fsdp", axis=1, tiled=True),
     )
     raw, seen = scores_with(pieces[0])

time: 787 us -> 877 us (1.11)
  local copies, waits for them, and re-layouts: 51.7 us -> 84.7 us
  waiting for transfers between devices: 383 us -> 411 us
  starting transfers between devices: 0.82 us -> 17.6 us
  matrix products: 176 us -> 185 us
    ppermute x0 -> x7, waiting for transfers between devices: none -> 88 us  [ring_gather(): lax.ppermute(pieces[far - 1], axis, [(d, (d - 1) % ways) for d in range(w...]
    all_gather x1, waiting for transfers between devices: 37.4 us -> 0.01 us  [on_device(): lax.all_gather(key_flat, 'fsdp', axis=1, tiled=True)]
    unnamed x87 -> x118, local copies, waits for them, and re-layouts: 13.7 us -> 39.8 us
    all_gather x1, waiting for transfers between devices: 23.9 us -> 0.02 us  [on_device(): lax.all_gather(value_flat, 'fsdp', axis=1, tiled=True)]
    ppermute x0 -> x7, starting transfers between devices: none -> 17 us  [ring_gather(): lax.ppermute(pieces[far - 1], axis, [(d, (d - 1) % ways) for d in range(w...]
    dot_general x1 -> x2, matrix products: 12.9 us -> 23.4 us  [scores_with(): jnp.einsum('sqhd,skhd->shqk', query_low, keys, preferred_element_type=jnp...]
  transfers between devices with their start and end apart: 9 -> 16, of which waited for: 5 -> 10; matrix products, arithmetic and copies ran while one was open for 33% -> 34% of each run, Pallas kernels for 0% -> 0%
where the time goes in v1:
time: 877 us; the launch traced here: 867 us
  waiting for transfers between devices  411 us (47%)
  matrix products  185 us (21%)
  local copies, waits for them, and re-layouts  84.7 us (10%)
  blocking collectives  79.8 us (9%)
  other arithmetic  72.7 us (8%)
  starting transfers between devices  17.6 us (2%)
  between operations  16.4 us (2%)
    reduce_scatter x1, waiting for transfers between devices, on_device(): lax.psum_scatter(jnp.concatenate([jnp.einsum('rc,rk->ck', input_one, grad...  173 us
    ppermute x7, waiting for transfers between devices, ring_gather(): lax.ppermute(pieces[far - 1], axis, [(d, (d - 1) % ways) for d in range(w...  88 us
    reduce_scatter x1, waiting for transfers between devices, on_device(): lax.psum_scatter(key_terms, 'fsdp', scatter_dimension=1, tiled=True)  84.1 us
    psum x1, waiting for transfers between devices, on_device(): owned = lax.psum(owned, 'rep')  64.2 us
    psum x1, blocking collectives, on_device(): lax.psum((local_vectors[0], local_vectors[1], local_vectors[2], local_vec...  44.4 us
    unnamed x118, local copies, waits for them, and re-layouts  39.8 us
    unnamed x1, blocking collectives  26.5 us
    dot_general x2, matrix products, scores_with(): jnp.einsum('sqhd,skhd->shqk', query_low, keys, preferred_element_type=jnp...  23.4 us
  transfers between devices with their start and end apart: 16, of which 10 were waited for; matrix products, arithmetic and copies ran while one was open for 34% of the time, Pallas kernels for 0%

profile of v1, /device:TPU:0, one launch (start us, length us, event | category | flops | bytes accessed | tf_op | source)
XLA Modules:
  0.0 867.5 jit_solution(344869509888427410)
XLA Ops:
  21.0 26.5 %all-reduce.19 = (bf16[768]{0:T(1024)(128)(2,1)S(1)}, bf16[768]{0:T(1024)(128)(2,1)S(1)}, bf16[768]{0:T(1024)(128)(2,1)}, bf16[768]{0:T(1024)(128)(2,1)}, bf16[7...) all-reduce(bf16[768]{0:T(1024)(128)(2,1)S(1)} %dynamic-update-slice, ...), channel_id=1, replica_groups=mesh['rep'=4,'fsdp'=8] {'fsdp'}, use_global_device_ids=true, to_apply=%add.15 | all-reduce | flops 6912 | bytes 27648
  77.0 16.3 %collective-permute-done = bf16[4,128,768]{1,2,0:T(8,128)(2,1)S(1)} collective-permute-done((bf16[4,128,768]{1,2,0:T(8,128)(2,1)}, bf16[4,128,768]{1,2,0:T(8,128)(2,1)S(1)}, u32[]{:S(2)}, u32[]{:S(2)}) %collective-permute-start) | collective-permute-done | bytes 786464 | tf_op jit(solution)/shard_map/ppermute | solution.py:18
  96.1 9.5 %collective-permute-done.1 = bf16[4,128,768]{1,2,0:T(8,128)(2,1)S(1)} collective-permute-done((bf16[4,128,768]{1,2,0:T(8,128)(2,1)S(1)}, bf16[4,128,768]{1,2,0:T(8,128)(2,1)S(1)}, u32[]{:S(2)}, u32[]{:S(2)}) %collective-permute-start.1) | collective-permute-done | bytes 786464 | tf_op jit(solution)/shard_map/ppermute | solution.py:18
  109.3 26.1 %collective-permute-done.2 = bf16[4,128,768]{1,2,0:T(8,128)(2,1)S(1)} collective-permute-done((bf16[4,128,768]{1,2,0:T(8,128)(2,1)S(1)}, bf16[4,128,768]{1,2,0:T(8,128)(2,1)S(1)}, u32[]{:S(2)}, u32[]{:S(2)}) %collective-permute-start.2) | collective-permute-done | bytes 786464 | tf_op jit(solution)/shard_map/ppermute | solution.py:18
  139.1 9.5 %collective-permute-done.3 = bf16[4,128,768]{1,2,0:T(8,128)(2,1)} collective-permute-done((bf16[4,128,768]{1,2,0:T(8,128)(2,1)S(1)}, bf16[4,128,768]{1,2,0:T(8,128)(2,1)}, u32[]{:S(2)}, u32[]{:S(2)}) %collective-permute-start.3) | collective-permute-done | bytes 786464 | tf_op jit(solution)/shard_map/ppermute | solution.py:18
  151.6 16.9 %collective-permute-done.4 = bf16[4,128,768]{1,2,0:T(8,128)(2,1)} collective-permute-done((bf16[4,128,768]{1,2,0:T(8,128)(2,1)}, bf16[4,128,768]{1,2,0:T(8,128)(2,1)}, u32[]{:S(2)}, u32[]{:S(2)}) %collective-permute-start.4) | collective-permute-done | bytes 786464 | tf_op jit(solution)/shard_map/ppermute | solution.py:18
  222.6 10.6 %fusion.68 = f32[4,12,128,1024]{3,2,1,0:T(8,128)} fusion(bf16[4,1024,12,64]{1,3,2,0:T(8,128)(2,1)S(1)} %bitcast.168, bf16[4,128,12,48]{1,3,2,0:T(8,128)(2,1)S(1)} %slice.110, bf16[4,128,12,16]{1,3,2,0:T(8,128)(2,1)S(1)} %copy-done.9), kind=kOutput, calls=%fused_computation.123 | convolution fusion | flops 806879232 | bytes 32243712 | tf_op jit(solution)/shard_map/sqhd,skhd->shqk/dot_general | solution.py:118
  233.2 12.8 %select_reduce_fusion.1 = (f32[4,12,128]{2,1,0:T(8,128)S(1)}, f32[4,12,128,1024]{3,2,1,0:T(8,128)}) fusion(pred[4,128,1024]{2,1,0:T(8,128)(4,1)S(1)} %fusion.26, bf16[4,1024,12,64]{1,3,2,0:T(8,128)(2,1)} %bitcast.166, bf16[4,128,12,48]{1,3,2,0:T(8,128)(2,1)S(1)} %slice.110, bf16[4,128,12,16]{1,3,2,0:T(8,128)(2,1)S(1)} %copy-done.9), kind=kOutput, calls=%fused_computation.7 | convolution fusion | flops 825747456 | bytes 32792576 | tf_op jit(solution)/shard_map/sqhd,skhd->shqk/dot_general | solution.py:118
  246.1 12.2 %select_reduce_fusion = f32[4,12,128]{2,1,0:T(8,128)S(1)} fusion(f32[4,12,128,1024]{3,2,1,0:T(8,128)} %get-tuple-element.76, f32[4,12,128]{2,1,0:T(8,128)S(1)} %broadcast_maximum_fusion, pred[4,128,1024]{2,1,0:T(8,128)(4,1)S(1)} %fusion.26), kind=kLoop, calls=%fused_computation.6 | loop fusion | flops 31451136 | bytes 25739264 | tf_op jit(solution)/shard_map/reduce_sum | solution.py:132
  258.4 14.1 %fusion.2 = f32[4,12,64,128]{3,2,1,0:T(8,128)} fusion(bf16[4,1024,12,64]{1,3,2,0:T(8,128)(2,1)} %bitcast.196, f32[4,12,128,1024]{3,2,1,0:T(8,128)} %fusion.68, f32[4,12,128]{2,1,0:T(8,128)S(1)} %log_add_fusion, pred[4,128,1024]{2,1,0:T(8,128)(4,1)S(1)} %fusion.26), kind=kOutput, calls=%fused_computation.10 | convolution fusion | flops 830472192 | bytes 33579008 | tf_op jit(solution)/shard_map/shqk,skhd->sqhd/dot_general | solution.py:144
  272.4 15.5 %fusion.29 = f32[4,128,12]{1,2,0:T(8,128)S(1)} fusion(f32[4,12,64,128]{3,2,1,0:T(8,128)} %fusion.2, bf16[4,1024,12,64]{1,3,2,0:T(8,128)(2,1)} %bitcast.197, f32[4,12,128,1024]{3,2,1,0:T(8,128)} %fusion.68, f32[4,12,128]{2,1,0:T(8,128)S(1)} %log_add_fusion, pred[4,128,1024]{2,1,0:T(8,128)(4,1)S(1)} %fusion.26, bf16[4,128,12,64]{1,0,3,2:T(4,128)(2,1)} %reshape.257), kind=kOutput, calls=%fused_computation.60 | convolution fusion | flops 850913280 | bytes 34390016 | tf_op jit(solution)/shard_map/shqk,skhd->sqhd/dot_general | solution.py:145
  287.9 20.4 %multiply_convert_fusion = bf16[4,12,128,1024]{3,2,1,0:T(8,128)(2,1)} fusion(f32[4,12,128,1024]{3,2,1,0:T(8,128)} %get-tuple-element.76, f32[4,12,128]{2,1,0:T(8,128)S(1)} %bitcast.200, f32[4,12,128]{2,1,0:T(8,128)S(1)} %log_add_fusion, pred[4,128,1024]{2,1,0:T(8,128)(4,1)S(1)} %fusion.26, bf16[4,1024,12,64]{1,3,2,0:T(8,128)(2,1)} %bitcast.198, ...), kind=kOutput, calls=%fused_computation.2 | convolution fusion | flops 843055104 | bytes 45400064 | tf_op jit(solution)/shard_map/sqhd,skhd->shqk/dot_general | solution.py:183
  308.3 10.9 %fusion.66 = f32[4,12,64,1024]{3,2,1,0:T(8,128)} fusion(bf16[4,12,128,1024]{3,2,1,0:T(8,128)(2,1)} %multiply_convert_fusion, bf16[4,128,12,48]{1,3,2,0:T(8,128)(2,1)S(1)} %slice.110, bf16[4,128,12,16]{1,3,2,0:T(8,128)(2,1)S(1)} %copy-done.9), kind=kOutput, calls=%fused_computation.121 | convolution fusion | flops 806879232 | bytes 25952256 | tf_op jit(solution)/shard_map/shqk,sqhd->skhd/dot_general | solution.py:190
  319.2 13.6 %fusion.4 = f32[4,12,64,1024]{3,2,1,0:T(8,128)} fusion(f32[4,12,128,1024]{3,2,1,0:T(8,128)} %get-tuple-element.76, f32[4,12,128]{2,1,0:T(8,128)S(1)} %log_add_fusion, pred[4,128,1024]{2,1,0:T(8,128)(4,1)S(1)} %fusion.26, bf16[4,128,12,64]{1,0,3,2:T(4,128)(2,1)S(1)} %copy-done.20), kind=kOutput, calls=%fused_computation.11 | convolution fusion | flops 830472192 | bytes 39084032 | tf_op jit(solution)/shard_map/shqk,sqhd->skhd/dot_general | solution.py:193
  332.9 18.7 %pad_maximum_fusion.1 = f32[4,1024,1536]{1,2,0:T(8,128)} fusion(f32[4,1024,768]{1,2,0:T(8,128)} %bitcast.165, f32[4,1024,768]{1,2,0:T(8,128)} %bitcast.164), kind=kLoop, calls=%fused_computation.1 | loop fusion | flops 6291456 | bytes 50331648 | tf_op jit(solution)/shard_map/concatenate | solution.py:196
  352.3 8.9 %all-gather = bf16[8,1,384]{2,1,0:T(2,128)(2,1)S(1)} all-gather(bf16[1,1,384]{2,1,0:T(2,128)(2,1)S(1)} %reshape.283), channel_id=1, replica_groups=mesh['rep'=4,'fsdp'=8] {'fsdp'}, dimensions={0}, use_global_device_ids=true | all-gather | bytes 6912 | tf_op jit(solution)/shard_map/all_gather | solution.py:75
  362.5 8.9 %fusion.93 = f32[512,3072]{1,0:T(8,128)} fusion(bf16[512,768]{1,0:T(8,128)(2,1)S(1)} %get-tuple-element.54, bf16[768,3072]{1,0:T(8,128)(2,1)} %all-gather.16.cloned.1.call-done), kind=kOutput, calls=%fused_computation.183 | convolution fusion | flops 2415919104 | bytes 11796480 | tf_op jit(solution)/shard_map/dot_general | solution.py:92
  371.4 19.3 %convert_reduce_fusion = (f32[3072]{0:T(1024)S(1)}, bf16[512,3072]{1,0:T(8,128)(2,1)S(1)}, f32[512,3072]{1,0:T(8,128)S(1)}) fusion(f32[512,3072]{1,0:T(8,128)} %fusion.93, f32[3072]{0:T(1024)S(1)} %bitcast.194, bf16[512,768]{1,0:T(8,128)(2,1)S(1)} %bitcast.177, bf16[768,3072]{1,0:T(8,128)(2,1)} %all-gather.18.cloned.1.call-done), kind=kOutput, calls=%fused_computation.24 | convolution fusion | flops 2533880832 | bytes 21258240 | tf_op jit(solution)/shard_map/dot_general | solution.py:166
  406.3 11.6 %multiply_bitcast_fusion = f32[4,128,12,64]{1,3,2,0:T(8,128)S(1)} fusion(bf16[4,1024,12,64]{1,3,2,0:T(8,128)(2,1)} %bitcast.167, bf16[4,12,128,1024]{3,2,1,0:T(8,128)(2,1)} %multiply_convert_fusion), kind=kOutput, calls=%fused_computation.94 | convolution fusion | flops 805699584 | bytes 20447232 | tf_op jit(solution)/shard_map/shqk,skhd->sqhd/dot_general | solution.py:187
  426.0 84.1 %reduce-scatter.3.cloned.1.call-done = f32[4,128,1536]{1,2,0:T(8,128)} async-done(((f32[4,1024,1536]{1,2,0:T(8,128)}), f32[4,128,1536]{1,2,0:T(8,128)}) %reduce-scatter.3.cloned.1.call-update) | async-done | bytes 3145744 | tf_op jit(solution)/shard_map/reduce_scatter | solution.py:203
  522.9 19.4 %pad_maximum_fusion = f32[768,9216]{1,0:T(8,128)} fusion(f32[768,3072]{1,0:T(8,128)} %convolution_bitcast_fusion, f32[768,3072]{1,0:T(8,128)} %fusion.96, f32[768,768]{1,0:T(8,128)S(1)} %copy.57, f32[768,2304]{1,0:T(8,128)} %fusion.22), kind=kLoop, calls=%fused_computation | loop fusion | flops 21233664 | bytes 56623104 | tf_op jit(solution)/shard_map/concatenate | solution.py:250
  543.1 172.6 %reduce-scatter.5.cloned.1.call-done = f32[96,9216]{1,0:T(8,128)} async-done(((f32[768,9216]{1,0:T(8,128)}), f32[96,9216]{1,0:T(8,128)}) %reduce-scatter.5.cloned.1.call-update) | async-done | bytes 3538960 | tf_op jit(solution)/shard_map/reduce_scatter | solution.py:249
  737.6 44.4 %all-reduce.18 = (f32[768]{0:T(1024)S(1)}, f32[768]{0:T(1024)S(1)}, f32[768]{0:T(1024)S(1)}, f32[768]{0:T(1024)S(1)}, f32[2304]{0:T(1024)S(1)}, /*index=5*/f32[768]{0:T(1024)S(1)}, f32[3072]{0:T(1024)S(1)}) all-reduce(f32[768]{0:T(1024)S(1)} %get-tuple-element.23, ...), channel_id=1, replica_groups=mesh['rep'=4,'fsdp'=8] {'rep','fsdp'}, use_global_device_ids=true, to_apply=%region_13.14 | all-reduce | flops 9216 | bytes 73728 | tf_op jit(solution)/shard_map/psum | solution.py:231
  788.7 64.2 %all-reduce.22.cloned.1.call-done = f32[96,9216]{1,0:T(8,128)} async-done(((f32[96,9216]{1,0:T(8,128)}), f32[96,9216]{1,0:T(8,128)}) %all-reduce.22.cloned.1.call-update) | async-done | bytes 3538960 | tf_op jit(solution)/shard_map/psum | solution.py:263
  (232 shorter events, 184.1 us)
Async XLA Ops:
  7.2 42.0 %all-gather.8.cloned.1.call-start = ((), (), s32[]{:S(2)}) async-start(), calls=%async_computation.2 | async-start | bytes 3981312 | tf_op jit(solution)/shard_map/all_gather | solution.py:87
  7.9 164.0 %all-gather.14.cloned.1.call-start = ((), (), s32[]{:S(2)}) async-start(), calls=%async_computation.5 | async-start | bytes 1327104 | tf_op jit(solution)/shard_map/all_gather | solution.py:149
  8.7 224.6 %all-gather.12.cloned.1.call-start = ((), (), s32[]{:S(2)}) async-start(), calls=%async_computation.4 | async-start | bytes 7077888 | tf_op jit(solution)/shard_map/all_gather | solution.py:128
  11.6 349.7 %copy-start.35 = (f32[4,128]{1,0:T(4,128)}, f32[4,128]{1,0:T(4,128)S(1)}, u32[]{:S(2)}) copy-start(f32[4,128]{1,0:T(4,128)S(1)} %fusion.41) | copy-start | bytes 6148
  47.5 313.7 %copy-start.27 = (f32[768]{0:T(1024)}, f32[768]{0:T(1024)S(1)}, u32[]{:S(2)}) copy-start(f32[768]{0:T(1024)S(1)} %convert_element_type.128) | copy-start | bytes 9220
  70.5 101.5 %copy-start.6 = (bf16[4,128,768]{2,1,0:T(8,128)(2,1)S(1)}, bf16[4,128,768]{2,1,0:T(8,128)(2,1)}, u32[]{:S(2)}) copy-start(bf16[4,128,768]{2,1,0:T(8,128)(2,1)} %param.17) | copy-start | bytes 2359300
  73.5 184.9 %all-gather.10.cloned.1.call-start = ((), (), s32[]{:S(2)}) async-start(), calls=%async_computation.3 | async-start | bytes 7077888 | tf_op jit(solution)/shard_map/all_gather | solution.py:136
  75.2 105.9 %copy-start.3 = (bf16[4,128,12,64]{1,3,2,0:T(8,128)(2,1)S(1)}, bf16[4,128,12,64]{1,3,2,0:T(8,128)(2,1)}, u32[]{:S(2)}) copy-start(bf16[4,128,12,64]{1,3,2,0:T(8,128)(2,1)} %pad_maximum_fusion.3) | copy-start | bytes 2359300
  76.3 286.2 %all-gather.16.cloned.1.call-start = ((), (), s32[]{:S(2)}) async-start(), calls=%async_computation.6 | async-start | bytes 5308416 | tf_op jit(solution)/shard_map/all_gather | solution.py:88
  76.9 294.5 %all-gather.18.cloned.1.call-start = ((), (), s32[]{:S(2)}) async-start(), calls=%async_computation.7 | async-start | bytes 5308416 | tf_op jit(solution)/shard_map/all_gather | solution.py:150
  77.0 16.4 %collective-permute-start = (bf16[4,128,768]{1,2,0:T(8,128)(2,1)}, bf16[4,128,768]{1,2,0:T(8,128)(2,1)S(1)}, u32[]{:S(2)}, u32[]{:S(2)}) collective-permute-start(bf16[4,128,768]{1,2,0:T(8,128)(2,1)} %bitcast.170), channel_id=1, source_target_pairs={{0,7},{1,0},{2,1},{3,2},{4,3},{5,4},{6,5},{7,6},{8,15},{9,8},{10,9... | collective-permute-start | bytes 2359304 | tf_op jit(solution)/shard_map/ppermute | solution.py:18
  93.3 78.2 %copy-start.10 = (bf16[4,128,768]{1,2,0:T(8,128)(2,1)}, bf16[4,128,768]{1,2,0:T(8,128)(2,1)S(1)}, u32[]{:S(2)}) copy-start(bf16[4,128,768]{1,2,0:T(8,128)(2,1)S(1)} %collective-permute-done) | copy-start | bytes 2359300
  93.3 12.3 %collective-permute-start.1 = (bf16[4,128,768]{1,2,0:T(8,128)(2,1)S(1)}, bf16[4,128,768]{1,2,0:T(8,128)(2,1)S(1)}, u32[]{:S(2)}, u32[]{:S(2)}) collective-permute-start(bf16[4,128,768]{1,2,0:T(8,128)(2,1)S(1)} %collective-permute-done), channel_id=1, source_target_pairs={{0,7},{1,0},{2,1},{3,2},{4,3},{5,4},{6,5},{7,6},{8,15},{9,8},{10,9... | collective-permute-start | bytes 2359304 | tf_op jit(solution)/shard_map/ppermute | solution.py:18
  106.5 28.9 %collective-permute-start.2 = (bf16[4,128,768]{1,2,0:T(8,128)(2,1)S(1)}, bf16[4,128,768]{1,2,0:T(8,128)(2,1)S(1)}, u32[]{:S(2)}, u32[]{:S(2)}) collective-permute-start(bf16[4,128,768]{1,2,0:T(8,128)(2,1)S(1)} %collective-permute-done.1), channel_id=1, source_target_pairs={{0,7},{1,0},{2,1},{3,2},{4,3},{5,4},{6,5},{7,6},{8,15},{9,8},{10,9... | collective-permute-start | bytes 2359304 | tf_op jit(solution)/shard_map/ppermute | solution.py:18
  136.3 12.3 %collective-permute-start.3 = (bf16[4,128,768]{1,2,0:T(8,128)(2,1)S(1)}, bf16[4,128,768]{1,2,0:T(8,128)(2,1)}, u32[]{:S(2)}, u32[]{:S(2)}) collective-permute-start(bf16[4,128,768]{1,2,0:T(8,128)(2,1)S(1)} %collective-permute-done.2), channel_id=1, source_target_pairs={{0,7},{1,0},{2,1},{3,2},{4,3},{5,4},{6,5},{7,6},{8,15},{9,8},{10,9... | collective-permute-start | bytes 2359304 | tf_op jit(solution)/shard_map/ppermute | solution.py:18
  148.6 19.9 %collective-permute-start.4 = (bf16[4,128,768]{1,2,0:T(8,128)(2,1)}, bf16[4,128,768]{1,2,0:T(8,128)(2,1)}, u32[]{:S(2)}, u32[]{:S(2)}) collective-permute-start(bf16[4,128,768]{1,2,0:T(8,128)(2,1)} %collective-permute-done.3), channel_id=1, source_target_pairs={{0,7},{1,0},{2,1},{3,2},{4,3},{5,4},{6,5},{7,6},{8,15},{9,8},{10,9... | collective-permute-start | bytes 2359304 | tf_op jit(solution)/shard_map/ppermute | solution.py:18
  151.6 358.5 %reduce-scatter.3.cloned.1.call-start = ((), (), s32[]{:S(2)}) async-start(), calls=%async_computation.8 | async-start | bytes 28311552 | tf_op jit(solution)/shard_map/reduce_scatter | solution.py:203
  168.5 18.4 %collective-permute-start.5 = (bf16[4,128,768]{1,2,0:T(8,128)(2,1)}, bf16[4,128,768]{1,2,0:T(8,128)(2,1)}, u32[]{:S(2)}, u32[]{:S(2)}) collective-permute-start(bf16[4,128,768]{1,2,0:T(8,128)(2,1)} %collective-permute-done.4), channel_id=1, source_target_pairs={{0,7},{1,0},{2,1},{3,2},{4,3},{5,4},{6,5},{7,6},{8,15},{9,8},{10,9... | collective-permute-start | bytes 2359304 | tf_op jit(solution)/shard_map/ppermute | solution.py:18
  186.8 19.6 %collective-permute-start.6 = (bf16[4,128,768]{1,2,0:T(8,128)(2,1)}, bf16[4,128,768]{1,2,0:T(8,128)(2,1)S(1)}, u32[]{:S(2)}, u32[]{:S(2)}) collective-permute-start(bf16[4,128,768]{1,2,0:T(8,128)(2,1)} %collective-permute-done.5), channel_id=1, source_target_pairs={{0,7},{1,0},{2,1},{3,2},{4,3},{5,4},{6,5},{7,6},{8,15},{9,8},{10,9... | collective-permute-start | bytes 2359304 | tf_op jit(solution)/shard_map/ppermute | solution.py:18
  351.6 364.1 %reduce-scatter.5.cloned.1.call-start = ((), (), s32[]{:S(2)}) async-start(), calls=%async_computation.9 | async-start | bytes 31850496 | tf_op jit(solution)/shard_map/reduce_scatter | solution.py:249
  423.7 88.5 %copy-start.26 = (f32[4,128,16]{1,2,0:T(8,128)S(1)}, f32[4,128,16]{1,2,0:T(8,128)}, u32[]{:S(2)}) copy-start(f32[4,128,16]{1,2,0:T(8,128)} %copy-done.25) | copy-start | bytes 98308
  426.0 86.7 %copy-start.24 = (f32[4,128,16]{1,2,0:T(8,128)S(1)}, f32[4,128,16]{1,2,0:T(8,128)}, u32[]{:S(2)}) copy-start(f32[4,128,16]{1,2,0:T(8,128)} %copy-done.23) | copy-start | bytes 98308
  542.3 310.6 %all-reduce.22.cloned.1.call-start = ((), (), s32[]{:S(2)}) async-start(), calls=%async_computation.10 | async-start | bytes 7077888 | tf_op jit(solution)/shard_map/psum | solution.py:263
  782.0 78.0 %copy-start.41 = (f32[96]{0:T(128)}, f32[96]{0:T(128)S(1)}, u32[]{:S(2)}) copy-start(f32[96]{0:T(128)S(1)} %dynamic_slice.31) | copy-start | bytes 1156
  (35 other events, 350.0 us)
Sparse Core Ops, SparseCore 0:
  9.9 36.8 all-gather.7
  48.7 24.0 all-gather.13
  75.2 62.2 all-gather.11
  139.9 66.4 all-gather.9
  208.1 41.2 all-gather.15
  251.1 38.9 all-gather.17
  351.7 158.2 reduce-scatter.2
  542.4 173.2 reduce-scatter.4
  718.1 134.7 all-reduce.21
